TPU v7x, 256 devices: a whole 4x4x8 slice. The times are simulated.
256 devices in a mesh: section: 4 (over z_lo, core), mp: 64 (over y, z_hi, x).
Axes of the slice: x: 4, y: 4, z: 8 (z_hi: 4, z_lo: 2; z = z_hi * 2 + z_lo), core: 2. Of those that a mesh axis runs over, the one named last changes fastest.
Arguments:
- query_rows: bfloat16 [32768, 3200], P(('mp', 'section')), may hold values from -4.5 to 4.5
- key_rows: bfloat16 [32768, 3200], P(('mp', 'section')), may hold values from -4.5 to 4.5
- value_rows: bfloat16 [32768, 3200], P(('mp', 'section')), may hold values from -6 to 6
- image_lengths: int32 [32, 3], replicated, may hold values from 1 to 512, 1024 in all within a row
- dest_group: int32 [32768, 1], P(('mp', 'section')), may hold values from 0 to 3; in each aligned block of 128 rows (0 to 127, 128 to 255, ...) at most 64 rows name the same one
- proj_weight: bfloat16 [3200, 8192], P('mp', 'section'), may hold values from -0.109375 to 0.109375
- llm_grad: bfloat16 [4, 16384, 8192], P('section', 'mp'), may hold values from -6 to 6
Outputs:
- visual_embeds: bfloat16 [4, 16384, 8192], P('section', 'mp')
- visual_grad: bfloat16 [32768, 3200], P(('mp', 'section'))
Inputs may be any that keep to these rules, and one draw needn't show every extreme that they name: `image_lengths`: the entries of each block sum to 1024; each block has one image of exactly half of 1024 patches. `dest_group`: among the rows of one device (128 consecutive rows) no group is named by more than 64 rows, and in every draw some group is named by exactly 64 rows of some device.
All inputs are finite; a program needn't handle non-finite values.
Results may differ from a plain program's by a relative error of at most 0.0057.
Values may be sent and summed in bfloat16 or wider, within the bound.
A program may use at most 128 MiB of HBM per device.

v0:
```python
import jax
import jax.numpy as jnp
from jax import lax
from jax.sharding import PartitionSpec as P

DV = 3200
HEADS = 25
HEAD_DIM = 128
BLOCK = 1024


def swapped(value, axis, stride):
    return lax.ppermute(value, axis, [(i, i ^ 1 << stride) for i in range(lax.axis_size(axis))])


def image_index(img_lengths, rows_count):
    positions = jnp.arange(rows_count, dtype=jnp.int32)
    ends = jnp.cumsum(img_lengths)
    return jnp.sum((positions[:, None] >= ends[None, :]).astype(jnp.int32), axis=1)


def attend_heads(packed, img_lengths):
    rows_count = packed.shape[1]
    head_count = packed.shape[2] // HEAD_DIM
    segment = image_index(img_lengths, rows_count)
    same_image = segment[:, None] == segment[None, :]
    heads = packed.reshape(3, rows_count, head_count, HEAD_DIM).transpose(2, 0, 1, 3)

    def one_head(triple):
        scores = jnp.dot(triple[0], triple[1].T, preferred_element_type=jnp.float32) * HEAD_DIM ** (
            -0.5
        )
        scores = jnp.where(same_image, scores, -1e30)
        row_max = jnp.max(scores, axis=1, keepdims=True)
        raised = jnp.exp(scores - row_max)
        totals = jnp.sum(raised, axis=1, keepdims=True)
        weights_bf = (raised / totals).astype(jnp.bfloat16)
        return jnp.dot(weights_bf, triple[2], preferred_element_type=jnp.float32).astype(
            jnp.bfloat16
        )

    mixed = lax.map(one_head, heads)
    return mixed.transpose(1, 0, 2).reshape(rows_count, head_count * HEAD_DIM)


def pick_half(data, own_bit):
    staying = lax.dynamic_index_in_dim(data, own_bit, 1, keepdims=False)
    leaving = lax.dynamic_index_in_dim(data, 1 - own_bit, 1, keepdims=False)
    return (staying, leaving)


def join_rows(staying, arrived, own_bit):
    low_first = jnp.concatenate([staying, arrived], axis=2)
    high_first = jnp.concatenate([arrived, staying], axis=2)
    return jnp.where(own_bit == 0, low_first, high_first)


def join_groups(staying, arrived, own_bit):
    low_first = jnp.stack([staying, arrived], axis=1)
    high_first = jnp.stack([arrived, staying], axis=1)
    joined = jnp.where(own_bit == 0, low_first, high_first)
    return joined.reshape((joined.shape[0] * 2,) + joined.shape[2:])


def to_heads(packed, local_index, section_bits):
    for bit_pos in range(section_bits):
        own_bit = local_index >> bit_pos & 1
        halves = packed.reshape((packed.shape[0] // 2, 2) + packed.shape[1:])
        staying, leaving = pick_half(halves, own_bit)
        arrived = swapped(leaving, "section", bit_pos)
        packed = join_rows(staying, arrived, own_bit)
    bit_pos = 0
    own_bit = local_index >> section_bits + bit_pos & 1
    halves = packed.reshape((packed.shape[0] // 2, 2) + packed.shape[1:])
    staying, leaving = pick_half(halves, own_bit)
    arrived = swapped(leaving, "mp", bit_pos)
    packed = join_rows(staying, arrived, own_bit)
    return packed


def to_rows(mixed, local_index, section_bits, mp_bits):
    for bit_pos in reversed(range(mp_bits)):
        own_bit = local_index >> section_bits + bit_pos & 1
        halves = mixed.reshape(mixed.shape[0], 2, mixed.shape[1] // 2, mixed.shape[2])
        staying, leaving = pick_half(halves, own_bit)
        arrived = swapped(leaving, "mp", bit_pos)
        mixed = join_groups(staying, arrived, own_bit)
    for bit_pos in reversed(range(section_bits)):
        own_bit = local_index >> bit_pos & 1
        halves = mixed.reshape(mixed.shape[0], 2, mixed.shape[1] // 2, mixed.shape[2])
        staying, leaving = pick_half(halves, own_bit)
        arrived = swapped(leaving, "section", bit_pos)
        mixed = join_groups(staying, arrived, own_bit)
    return mixed


def slot_matrix(dest_col, groups, capacity):
    dest_ids = dest_col[:, 0]
    onehot = (dest_ids[:, None] == jnp.arange(groups, dtype=jnp.int32)[None, :]).astype(jnp.int32)
    earlier = jnp.cumsum(onehot, axis=0) - onehot
    slot_ids = jnp.sum(earlier * onehot, axis=1)
    target = dest_ids * capacity + slot_ids
    slots = jnp.arange(groups * capacity, dtype=jnp.int32)
    return (slots[:, None] == target[None, :]).astype(jnp.bfloat16)


def on_device(query_rows, key_rows, value_rows, image_lengths, dest_group, proj_weight, llm_grad):
    groups = lax.axis_size("section")
    block_rows = query_rows.shape[0]
    group_span = BLOCK // block_rows
    section_bits = groups.bit_length() - 1
    mp_bits = (group_span // groups).bit_length() - 1
    flat_index = lax.axis_index("mp") * groups + lax.axis_index("section")
    local_index = flat_index % group_span
    lengths_here = lax.dynamic_index_in_dim(
        image_lengths, flat_index // group_span, 0, keepdims=False
    )
    slot_heads = (HEADS + group_span - 1) // group_span
    padded_cols = group_span * slot_heads * HEAD_DIM
    packed = jnp.stack([query_rows, key_rows, value_rows])
    packed = jnp.pad(packed, ((0, 0), (0, 0), (0, padded_cols - DV)))
    packed = packed.reshape(3, block_rows, group_span, slot_heads * HEAD_DIM).transpose(2, 0, 1, 3)
    packed = to_heads(packed, local_index, section_bits)
    mixed = attend_heads(packed[0], lengths_here)
    spread = to_rows(mixed[None], local_index, section_bits, mp_bits)
    mixing = spread.transpose(1, 0, 2).reshape(block_rows, padded_cols)[:, :DV]
    capacity = llm_grad.shape[1] // groups
    full_cols = llm_grad.shape[2]
    tile_cols = proj_weight.shape[1]
    weight = lax.all_gather(proj_weight, "mp", axis=0, tiled=True)
    gathered = lax.all_gather(mixing, "section", axis=0, tiled=True)
    proj_tile = jnp.dot(gathered, weight, preferred_element_type=jnp.float32).astype(jnp.bfloat16)
    whole = lax.all_to_all(
        proj_tile.reshape(groups, block_rows, tile_cols),
        "section",
        split_axis=0,
        concat_axis=2,
        tiled=True,
    )
    whole = whole.reshape(block_rows, full_cols)
    placing = slot_matrix(dest_group, groups, capacity)
    outgoing = jnp.dot(placing, whole, preferred_element_type=jnp.float32).astype(jnp.bfloat16)
    arrived = lax.all_to_all(
        outgoing.reshape(groups, capacity, full_cols),
        "section",
        split_axis=0,
        concat_axis=0,
        tiled=True,
    )
    embeds = arrived.reshape(1, groups * capacity, full_cols)
    returned = lax.all_to_all(
        llm_grad.reshape(groups, capacity, full_cols),
        "section",
        split_axis=0,
        concat_axis=0,
        tiled=True,
    )
    own_grad = lax.dot_general(
        placing,
        returned.reshape(groups * capacity, full_cols),
        (((0,), (0,)), ((), ())),
        preferred_element_type=jnp.float32,
    ).astype(jnp.bfloat16)
    grad_tile = lax.all_to_all(own_grad, "section", split_axis=1, concat_axis=0, tiled=True)
    summed = lax.psum_scatter(
        lax.dot_general(
            grad_tile, weight, (((1,), (1,)), ((), ())), preferred_element_type=jnp.float32
        ),
        "section",
        scatter_dimension=0,
        tiled=True,
    )
    return (embeds, summed.astype(jnp.bfloat16))


def solution(mesh):
    placed = (
        P(("mp", "section"), None),
        P(("mp", "section"), None),
        P(("mp", "section"), None),
        P(),
        P(("mp", "section"), None),
        P("mp", "section"),
        P("section", "mp", None),
    )
    return jax.shard_map(
        on_device,
        mesh=mesh,
        in_specs=placed,
        out_specs=(P("section", "mp", None), P(("mp", "section"), None)),
        check_vma=False,
    )
```

profile of v0, /device:TPU:1, one launch (start us, length us, event | category | flops | bytes accessed | tf_op | source)
XLA Modules:
  0.0 449.2 jit_solution(10036131909588289699)
XLA Ops:
  14.9 3.2 copy.47
  20.1 3.2 collective-permute-start
  23.3 3.2 collective-permute-done
  30.8 58.8 %collective-permute-done.1 = bf16[2,3,256,512]{3,2,1,0:T(8,128)(2,1)S(1)} collective-permute-done((bf16[2,3,256,512]{3,2,1,0:T(8,128)(2,1)}, bf16[2,3,256,512]{3,2,1,0:T(8,128)(2,1)S(1)}, u32[]{:S(2)}, u32[]{:S(2)}) %collective-permute-start.1) | collective-permute-done | bytes 1572896 | tf_op jit(solution)/shard_map/ppermute | solution.py:13
  93.2 5.6 %all-to-all-start.2 = ((bf16[4,64,8192]{2,1,0:T(8,128)(2,1)}), bf16[4,64,8192]{2,1,0:T(8,128)(2,1)}, u32[]{:S(2)}, u32[]{:S(2)}) async-start(bf16[4,64,8192]{2,1,0:T(8,128)(2,1)} %bitcast.101), calls=%async_computation.2 | async-start | bytes 8388608 | tf_op jit(solution)/shard_map/all_to_all | solution.py:151
  100.1 47.1 %collective-permute-done.2 = bf16[1,3,512,512]{3,2,1,0:T(8,128)(2,1)} collective-permute-done((bf16[1,3,512,512]{3,2,1,0:T(8,128)(2,1)}, bf16[1,3,512,512]{3,2,1,0:T(8,128)(2,1)}, u32[]{:S(2)}, u32[]{:S(2)}) %collective-permute-start.2) | collective-permute-done | bytes 1572896 | tf_op jit(solution)/shard_map/ppermute | solution.py:13
  151.1 24.8 %while.11 = (s32[]{:T(128)}, bf16[4,1024,128]{2,1,0:T(8,128)(2,1)}, bf16[4,3,1024,128]{2,3,0,1:T(8,128)(2,1)}, s32[1024]{0:T(1024)S(1)}, s32[]{:T(128)}, /*index=5*/s32[]{:T(128)}, s32[]{}, s32[]{}) while((s32[]{:T(128)}, bf16[4,1024,128]{2,1,0:T(8,128)(2,1)}, bf16[4,3,1024,128]{2,3,0,1:T(8,128)(2,1)}, s32[1024]{0:T(1024)S(1)}, ...), condition=%wide.region_7.8_spmd.clone, body=%wide.region_4.7_spmd.clone.sunk | while | flops 552728576 | bytes 13675637 | solution.py:42
  154.0 3.2 fusion.35
  160.2 3.2 fusion.35
  166.4 3.3 fusion.35
  172.6 3.3 fusion.35
  181.0 12.2 %collective-permute-done.3 = bf16[1,512,512]{2,1,0:T(8,128)(2,1)S(1)} collective-permute-done((bf16[1,512,512]{2,1,0:T(8,128)(2,1)S(1)}, bf16[1,512,512]{2,1,0:T(8,128)(2,1)S(1)}, u32[]{:S(2)}, u32[]{:S(2)}) %collective-permute-start.3) | collective-permute-done | bytes 524320 | tf_op jit(solution)/shard_map/ppermute | solution.py:13
  193.4 7.4 %collective-permute-start.4 = (bf16[2,256,512]{2,1,0:T(8,128)(2,1)S(1)}, bf16[2,256,512]{2,1,0:T(8,128)(2,1)S(1)}, u32[]{:S(2)}, u32[]{:S(2)}) collective-permute-start(bf16[2,256,512]{2,1,0:T(8,128)(2,1)S(1)} %get-tuple-element.75), channel_id=1, source_target_pairs={{0,128},{64,192},{128,0},{192,64},{1,129},{65,193},{129,1},{193,65... | collective-permute-start | bytes 1572872 | tf_op jit(solution)/shard_map/ppermute | solution.py:13
  200.8 33.4 %collective-permute-done.4 = bf16[2,256,512]{2,1,0:T(8,128)(2,1)S(1)} collective-permute-done((bf16[2,256,512]{2,1,0:T(8,128)(2,1)S(1)}, bf16[2,256,512]{2,1,0:T(8,128)(2,1)S(1)}, u32[]{:S(2)}, u32[]{:S(2)}) %collective-permute-start.4) | collective-permute-done | bytes 524320 | tf_op jit(solution)/shard_map/ppermute | solution.py:13
  238.3 2.9 convolution_convert_fusion.1
  242.7 4.0 all-to-all-start.3
  246.7 17.1 %reshape.154 = bf16[3200,2048]{1,0:T(8,128)(2,1)} reshape(bf16[64,50,2048]{2,1,0:T(8,128)(2,1)} %all-gather.6.cloned.1.call-done) | data formatting | bytes 26214400
  263.7 24.6 %all-to-all-done.3 = bf16[128,4,2048]{2,0,1:T(8,128)(2,1)S(1)} async-done(((bf16[128,4,2048]{2,0,1:T(8,128)(2,1)}), bf16[128,4,2048]{2,0,1:T(8,128)(2,1)S(1)}, u32[]{:S(2)}, u32[]{:S(2)}) %all-to-all-start.3) | async-done | bytes 2097184 | tf_op jit(solution)/shard_map/all_to_all | solution.py:164
  288.3 12.6 %fusion.23 = f32[512,3200]{1,0:T(8,128)} fusion(bf16[512,2048]{1,0:T(8,128)(2,1)S(1)} %bitcast.107, bf16[3200,2048]{1,0:T(8,128)(2,1)} %reshape.154), kind=kOutput, calls=%fused_computation.58 | convolution fusion | flops 6710886400 | bytes 21757952 | tf_op jit(solution)/shard_map/dot_general | solution.py:166
  301.0 12.2 %convolution_convert_fusion.2 = bf16[512,2048]{1,0:T(8,128)(2,1)} fusion(bf16[512,3200]{0,1:T(8,128)(2,1)} %all-gather.4.cloned.1.call-done, bf16[3200,2048]{1,0:T(8,128)(2,1)} %reshape.154), kind=kOutput, calls=%fused_computation.30 | convolution fusion | flops 6711934976 | bytes 18481152 | tf_op jit(solution)/shard_map/dot_general | solution.py:132
  313.2 3.3 copy.53
  316.5 51.8 %all_to_all.44 = bf16[4,128,2048]{1,2,0:T(8,128)(2,1)S(1)} all-to-all(bf16[4,128,2048]{1,2,0:T(8,128)(2,1)S(1)} %copy.53), channel_id=1, replica_groups=mesh['section'=4,'mp'=64] {'section'}, dimensions={0} | all-to-all | bytes 4194304 | tf_op jit(solution)/shard_map/all_to_all | solution.py:133
  369.5 66.0 %all_to_all.45 = bf16[4,64,8192]{2,1,0:T(8,128)(2,1)} all-to-all(bf16[4,64,8192]{2,1,0:T(8,128)(2,1)S(1)} %bitcast.92), channel_id=1, replica_groups=mesh['section'=4,'mp'=64] {'section'}, dimensions={0} | all-to-all | bytes 8388608 | tf_op jit(solution)/shard_map/all_to_all | solution.py:143
  438.0 4.6 %copy.70 = bf16[1,256,8192]{2,1,0:T(8,128)(2,1)} copy(bf16[1,256,8192]{2,1,0:T(8,128)(2,1)} %bitcast.91) | data formatting | bytes 8388608
  (64 shorter events, 48.9 us)
Async XLA Ops:
  7.2 91.7 %copy-start = (s32[32,3]{0,1:T(4,128)S(1)}, s32[32,3]{0,1:T(4,128)}, u32[]{:S(2)}) copy-start(s32[32,3]{0,1:T(4,128)} %param.12) | copy-start | bytes 1156
  7.2 4.2 copy-start.2
  7.2 239.5 %all-gather.6.cloned.1.call-start = ((), (), s32[]{:S(2)}) async-start(), calls=%async_computation.7 | async-start | bytes 14909440 | tf_op jit(solution)/shard_map/all_gather | solution.py:130
  20.1 6.5 %collective-permute-start = (bf16[4,3,128,512]{3,2,1,0:T(8,128)(2,1)}, bf16[4,3,128,512]{3,2,1,0:T(8,128)(2,1)S(1)}, u32[]{:S(2)}, u32[]{:S(2)}) collective-permute-start(bf16[4,3,128,512]{3,2,1,0:T(8,128)(2,1)} %get-tuple-element.71), channel_id=1, source_target_pairs={{0,64},{64,0},{128,192},{192,128},{1,65},{65,1},{129,193},{193,129... | collective-permute-start | bytes 4718600 | tf_op jit(solution)/shard_map/ppermute | solution.py:13
  30.8 58.8 %collective-permute-start.1 = (bf16[2,3,256,512]{3,2,1,0:T(8,128)(2,1)}, bf16[2,3,256,512]{3,2,1,0:T(8,128)(2,1)S(1)}, u32[]{:S(2)}, u32[]{:S(2)}) collective-permute-start(bf16[2,3,256,512]{3,2,1,0:T(8,128)(2,1)} %get-tuple-element.69), channel_id=1, source_target_pairs={{0,128},{64,192},{128,0},{192,64},{1,129},{65,193},{129,1},{193,65... | collective-permute-start | bytes 4718600 | tf_op jit(solution)/shard_map/ppermute | solution.py:13
  92.0 55.1 %collective-permute-start.2 = (bf16[1,3,512,512]{3,2,1,0:T(8,128)(2,1)}, bf16[1,3,512,512]{3,2,1,0:T(8,128)(2,1)}, u32[]{:S(2)}, u32[]{:S(2)}) collective-permute-start(bf16[1,3,512,512]{3,2,1,0:T(8,128)(2,1)} %get-tuple-element.67), channel_id=1, source_target_pairs={{0,1},{1,0},{2,3},{3,2},{4,5},{5,4},{6,7},{7,6},{8,9},{9,8},{10,11... | collective-permute-start | bytes 4718600 | tf_op jit(solution)/shard_map/ppermute | solution.py:13
  93.2 145.1 %all-to-all-start.2 = ((bf16[4,64,8192]{2,1,0:T(8,128)(2,1)}), bf16[4,64,8192]{2,1,0:T(8,128)(2,1)}, u32[]{:S(2)}, u32[]{:S(2)}) async-start(bf16[4,64,8192]{2,1,0:T(8,128)(2,1)} %bitcast.101), calls=%async_computation.2 | async-start | bytes 8388608 | tf_op jit(solution)/shard_map/all_to_all | solution.py:151
  98.9 202.1 %all-gather.4.cloned.1.call-start = ((), (), s32[]{:S(2)}) async-start(), calls=%async_computation.5 | async-start | bytes 4096000 | tf_op jit(solution)/shard_map/all_gather | solution.py:131
  178.5 14.6 %collective-permute-start.3 = (bf16[1,512,512]{2,1,0:T(8,128)(2,1)S(1)}, bf16[1,512,512]{2,1,0:T(8,128)(2,1)S(1)}, u32[]{:S(2)}, u32[]{:S(2)}) collective-permute-start(bf16[1,512,512]{2,1,0:T(8,128)(2,1)S(1)} %get-tuple-element.77), channel_id=1, source_target_pairs={{0,1},{1,0},{2,3},{3,2},{4,5},{5,4},{6,7},{7,6},{8,9},{9,8},{10,11... | collective-permute-start | bytes 1572872 | tf_op jit(solution)/shard_map/ppermute | solution.py:13
  193.3 41.7 %copy-start.3 = (s32[128,1]{0,1:T(1,128)S(1)}, s32[128,1]{0,1:T(1,128)}, u32[]{:S(2)}) copy-start(s32[128,1]{0,1:T(1,128)} %param.13) | copy-start | bytes 1540
  193.4 40.7 %collective-permute-start.4 = (bf16[2,256,512]{2,1,0:T(8,128)(2,1)S(1)}, bf16[2,256,512]{2,1,0:T(8,128)(2,1)S(1)}, u32[]{:S(2)}, u32[]{:S(2)}) collective-permute-start(bf16[2,256,512]{2,1,0:T(8,128)(2,1)S(1)} %get-tuple-element.75), channel_id=1, source_target_pairs={{0,128},{64,192},{128,0},{192,64},{1,129},{65,193},{129,1},{193,65... | collective-permute-start | bytes 1572872 | tf_op jit(solution)/shard_map/ppermute | solution.py:13
  234.4 2.2 collective-permute-start.5
  242.7 45.6 %all-to-all-start.3 = ((bf16[128,4,2048]{2,0,1:T(8,128)(2,1)}), bf16[128,4,2048]{2,0,1:T(8,128)(2,1)S(1)}, u32[]{:S(2)}, u32[]{:S(2)}) async-start(bf16[128,4,2048]{2,0,1:T(8,128)(2,1)} %bitcast.82), calls=%async_computation.3 | async-start | bytes 4194304 | tf_op jit(solution)/shard_map/all_to_all | solution.py:164
  246.7 188.9 %reduce-scatter.2.cloned.1.call-start = ((), (), s32[]{:S(2)}) async-start(), calls=%async_computation.6 | async-start | bytes 8192000 | tf_op jit(solution)/shard_map/reduce_scatter | solution.py:165
  435.6 7.1 %copy-start.1 = (s32[32,3]{0,1:T(4,128)S(1)}, s32[32,3]{0,1:T(4,128)}, u32[]{:S(2)}) copy-start(s32[32,3]{0,1:T(4,128)} %param.12) | copy-start | bytes 1156
Sparse Core Ops, SparseCore 0:
  11.3 205.8 all-gather.5
  238.4 59.7 all-gather.3
  301.1 105.2 reduce-scatter.1
where the time goes:
time: 450 us; the launch traced here: 449 us
  waiting for transfers between devices  181 us (40%)
  blocking collectives  118 us (26%)
  matrix products  49.7 us (11%)
  local copies, waits for them, and re-layouts  45.6 us (10%)
  starting transfers between devices  24.6 us (5%)
  other arithmetic  16.4 us (4%)
  between operations  14 us (3%)
    ppermute x6, waiting for transfers between devices, swapped(): lax.ppermute(value, axis, [(i, i ^ 1 << stride) for i in range(lax.axis_s...  156 us
    all_to_all x1, blocking collectives, on_device(): lax.all_to_all(outgoing.reshape(groups, capacity, full_cols), 'section',...  66 us
    all_to_all x1, blocking collectives, on_device(): lax.all_to_all(proj_tile.reshape(groups, block_rows, tile_cols), 'section...  51.8 us
    unnamed x13, local copies, waits for them, and re-layouts  26 us
    all_to_all x1, waiting for transfers between devices, on_device(): lax.all_to_all(own_grad, 'section', split_axis=1, concat_axis=0, tiled=True)  24.6 us
    ppermute x6, starting transfers between devices, swapped(): lax.ppermute(value, axis, [(i, i ^ 1 << stride) for i in range(lax.axis_s...  14.9 us
    dot_general x4, matrix products, one_head(): jnp.dot(weights_bf, triple[2], preferred_element_type=jnp.float32)  13 us
    dot_general x1, matrix products, on_device(): lax.dot_general(grad_tile, weight, (((1,), (1,)), ((), ())), preferred_el...  12.6 us
  transfers between devices with their start and end apart: 11, of which 7 were waited for; matrix products, arithmetic and copies ran while one was open for 23% of the time, Pallas kernels for 0%

commit v1 on v0

v1 whole, which is shorter than its diff:
```python
import functools

import jax
import jax.numpy as jnp
from jax import lax
from jax.experimental import pallas as pl
from jax.experimental.pallas import tpu as pltpu
from jax.sharding import PartitionSpec as P

MESH = pl.DeviceIdType.MESH
BF = jnp.bfloat16
F32 = jnp.float32
HD = 128
BLOCK = 1024
TILE = 128
CAP = 64
DV = 3200
OWN = 384
LAST = 3072
ROWS = 400
COLS = 256
SIZES = {"x": 4, "y": 4, "z": 8}
PARTS = (
    (0, 48, "xyz", 0),
    (48, 48, "xyz", 0),
    (96, 32, "zxy", 1),
    (128, 64, "zyx", 0),
    (192, 64, "zyx", 0),
    (256, 80, "zxy", 0),
    (336, 64, "zxy", 1),
)
K_PARTS = ((0, 128, 0), (128, 128, 1024), (256, 128, 2048), (384, 16, 3072))


def place():
    section, mp = lax.axis_index("section"), lax.axis_index("mp")
    return {
        "x": mp % 4,
        "y": mp // 16,
        "z": ((mp // 4) % 4) * 2 + section // 2,
        "c": section % 2,
    }


def device(at):
    return {
        "mp": (at["y"] * 4 + at["z"] // 2) * 4 + at["x"],
        "section": (at["z"] % 2) * 2 + at["c"],
    }


def one_hot(condition):
    return jnp.where(condition, 1.0, 0.0).astype(BF)


def dot(a, b):
    return jnp.dot(a, b, preferred_element_type=F32)


def dot_nt(a, b):
    return lax.dot_general(a, b, (((1,), (1,)), ((), ())), preferred_element_type=F32)


def placing(dest):
    group = lax.broadcasted_iota(jnp.int32, (8, TILE), 0)
    named = jnp.where(group == dest, 1.0, 0.0)
    before = one_hot(
        lax.broadcasted_iota(jnp.int32, (TILE, TILE), 0)
        < lax.broadcasted_iota(jnp.int32, (TILE, TILE), 1)
    )
    earlier = dot(named.astype(BF), before)
    rank = jnp.sum(named * earlier, axis=0, keepdims=True)
    target = dest[0:1].astype(F32) * float(CAP) + rank
    slots = lax.broadcasted_iota(jnp.int32, (4 * CAP, TILE), 0).astype(F32)
    return jnp.where(slots == target, 1.0, 0.0)


def segments(shape, axis, start, ends):
    rows = lax.broadcasted_iota(jnp.int32, shape, axis) + start
    count = jnp.zeros(shape, jnp.int32)
    for end in ends:
        count = count + jnp.where(rows >= end, 1, 0)
    return count


def attend(q, k, v, same):
    scores = dot_nt(q, k) * HD ** (-0.5)
    scores = jnp.where(same, scores, -1e30)
    raised = jnp.exp(scores - jnp.max(scores, axis=1, keepdims=True))
    inverse = 1.0 / jnp.sum(raised, axis=1, keepdims=True)
    return dot((raised * inverse).astype(BF), v).astype(BF)


class Copies:
    def __init__(self, send, recv):
        self.send, self.recv, self.count, self.sent = send, recv, 0, []

    def new(self):
        self.count += 1
        return self.count - 1

    def make(self, index, src, dst, to):
        return pltpu.make_async_remote_copy(
            src_ref=src,
            dst_ref=dst,
            send_sem=self.send.at[index],
            recv_sem=self.recv.at[index],
            device_id=to,
            device_id_type=MESH,
        )

    def start(self, index, src, dst, to):
        copy = self.make(index, src, dst, to)
        copy.start()
        self.sent.append(copy)
        return copy

    def arrive(self, index, dst, to):
        self.make(index, dst, dst, to).wait_recv()

    def drain(self):
        for copy in self.sent:
            copy.wait_send()
        self.sent = []


def ring(copies, buf, me, part):
    first, rows, order, flip = part
    done = []
    for axis in order:
        size = SIZES[axis]
        even = 1 - 2 * (me[axis] % 2)
        step = -even if flip else even
        near = {**me, axis: (me[axis] + step + size) % size}
        far = {**me, axis: (me[axis] - step + size) % size}

        def block(offset):
            at = {
                **{a: me[a] for a in SIZES},
                axis: (me[axis] + offset * step + size) % size,
            }
            index = []
            for a in ("y", "z", "x"):
                if a in done:
                    index += [slice(None)] * (2 if a == "z" else 1)
                elif a == "z":
                    index += [at[a] // 4, at[a] % 4]
                else:
                    index += [at[a]]
            return buf.at[(*index, pl.ds(first, rows), slice(None))]

        to_far = [copies.new() for _ in range(size // 2)]
        to_near = [copies.new() for _ in range(size // 2 - 1)]
        copies.start(to_far[0], block(0), block(0), device(far))
        copies.start(to_near[0], block(0), block(0), device(near))
        for k in range(size // 2):
            yield
            if k < size // 2 - 1:
                copies.arrive(to_near[k], block(k + 1), device(near))
                copies.start(to_far[k + 1], block(k + 1), block(k + 1), device(far))
            copies.arrive(to_far[k], block(-(k + 1)), device(far))
            if k + 1 < size // 2 - 1:
                copies.start(
                    to_near[k + 1], block(-(k + 1)), block(-(k + 1)), device(near)
                )
        done = done + [axis]


def kernel(
    lengths,
    dest_ref,
    q_ref,
    k_ref,
    v_ref,
    w_ref,
    grad_ref,
    embeds_ref,
    vgrad_ref,
    weight,
    w_pieces,
    qkv,
    kv_last,
    q_last,
    dests,
    mixed,
    staged,
    staged_last,
    slots,
    lhs,
    grads,
    embeds,
    back,
    back_in,
    returned,
    send_sem,
    recv_sem,
    local_sem,
):
    me = place()
    section, mp = lax.axis_index("section"), lax.axis_index("mp")
    core = me["c"]
    local = (mp % 2) * 4 + section
    member = mp % 8
    copies = Copies(send_sem, recv_sem)
    sibling = device({**me, "c": 1 - core})

    def in_block(index):
        return {"mp": mp - mp % 2 + index // 4, "section": index % 4}

    def in_octet(index):
        return {"mp": mp - mp % 8 + index, "section": section}

    def in_section(index):
        return {"mp": mp, "section": index}

    greeted = [in_block((local + k) % 8) for k in range(1, 8)]
    greeted += [in_octet((member + k) % 8) for k in range(1, 8)]
    for axis, size in SIZES.items():
        for step in (1, size - 1):
            greeted.append(device({**me, axis: (me[axis] + step) % size}))
    barrier = pltpu.get_barrier_semaphore()
    for other in greeted:
        pl.semaphore_signal(barrier, inc=1, device_id=other, device_id_type=MESH)
    pl.semaphore_wait(barrier, len(greeted))

    locals_ = []

    def local_copy(src, dst):
        copy = pltpu.make_async_copy(src, dst, local_sem.at[len(locals_)])
        copy.start()
        locals_.append(copy)
        return copy

    piece_sems = [copies.new() for _ in range(7)]
    for k in range(1, 8):
        to = (member + k) % 8
        columns = pl.ds(pl.multiple_of(to * COLS, COLS), COLS)
        copies.start(
            piece_sems[k - 1],
            w_ref.at[:, columns],
            w_pieces.at[member],
            in_octet(to),
        )
    columns = pl.ds(pl.multiple_of(member * COLS, COLS), COLS)
    piece_own = local_copy(w_ref.at[:, columns], w_pieces.at[member])

    head_sems = [[copies.new() for _ in range(6)] for _ in range(7)]
    last_columns = pl.ds(LAST, HD)
    for k in range(1, 8):
        to = (local + k) % 8
        columns = pl.ds(pl.multiple_of(to * OWN, HD), OWN)
        for i, ref in enumerate((q_ref, k_ref, v_ref)):
            copies.start(
                head_sems[k - 1][i],
                ref.at[:, columns],
                qkv.at[local, i],
                in_block(to),
            )
        for i, ref in enumerate((k_ref, v_ref)):
            copies.start(
                head_sems[k - 1][3 + i],
                ref.at[:, last_columns],
                kv_last.at[local, i],
                in_block(to),
            )
        copies.start(head_sems[k - 1][5], dest_ref, dests.at[local], in_block(to))
    columns = pl.ds(pl.multiple_of(local * OWN, HD), OWN)
    head_own = [
        local_copy(ref.at[:, columns], qkv.at[local, i])
        for i, ref in enumerate((q_ref, k_ref, v_ref))
    ]
    head_own += [
        local_copy(ref.at[:, last_columns], kv_last.at[local, i])
        for i, ref in enumerate((k_ref, v_ref))
    ]
    head_own.append(local_copy(q_ref.at[:, last_columns], q_last))
    head_own.append(local_copy(dest_ref, dests.at[local]))

    piece_own.wait()
    for k in range(1, 8):
        source = (member - k + 8) % 8
        copies.arrive(piece_sems[k - 1], w_pieces.at[source], in_octet(source))
    row = lax.broadcasted_iota(jnp.int32, (ROWS, 512), 0)
    column = lax.broadcasted_iota(jnp.int32, (ROWS, 512), 1)
    inner = column % 64
    choose = one_hot((row == (column // 64) * 50 + inner) & (inner < 50))
    tile = dot(choose, w_pieces[...].reshape(512, COLS)).astype(BF)
    weight[me["y"], me["z"] // 4, me["z"] % 4, me["x"]] = tile
    gathers = [ring(copies, weight, me, part) for part in PARTS]

    def advance():
        for gather in gathers:
            next(gather, None)

    advance()

    grad_sems = [copies.new() for _ in range(2)]
    for half in range(2):
        there = pl.ds(pl.multiple_of((2 * half + 1 - core) * 2048, 2048), 2048)
        here = pl.ds(pl.multiple_of((2 * half + core) * 2048, 2048), 2048)
        into = pl.ds(half * 2048, 2048)
        copies.start(
            grad_sems[half],
            grad_ref.at[0, :, there],
            grads.at[core, :, into],
            sibling,
        )
        local_copy(grad_ref.at[0, :, here], grads.at[core, :, into])
    grad_own = locals_[-2:]

    for _ in range(6):
        advance()

    for copy in head_own:
        copy.wait()
    for k in range(1, 8):
        source = (local - k + 8) % 8
        for i in range(3):
            copies.arrive(head_sems[k - 1][i], qkv.at[source, i], in_block(source))
        for i in range(2):
            copies.arrive(
                head_sems[k - 1][3 + i], kv_last.at[source, i], in_block(source)
            )
        copies.arrive(head_sems[k - 1][5], dests.at[source], in_block(source))
    block = mp // 2
    ends = []
    total = 0
    for i in range(3):
        total = total + lengths[block, i]
        ends.append(total)
    key_segments = segments((1, BLOCK), 1, 0, ends)

    def attend_chunk(i, carry):
        columns = pl.ds(pl.multiple_of((i // 4) * HD, HD), HD)
        tiles = pl.ds((i % 4) * 2, 2)
        q = qkv[tiles, 0, :, columns].reshape(2 * TILE, HD)
        k = qkv[:, 1, :, columns].reshape(BLOCK, HD)
        v = qkv[:, 2, :, columns].reshape(BLOCK, HD)
        same = segments((2 * TILE, 1), 0, (i % 4) * 2 * TILE, ends) == key_segments
        mixed[tiles, :, columns] = attend(q, k, v, same).reshape(2, TILE, HD)
        return carry

    for head in range(3):
        lax.fori_loop(4 * head, 4 * head + 4, attend_chunk, 0)
    same = segments((TILE, 1), 0, local * TILE, ends) == key_segments
    last = attend(
        q_last[...],
        kv_last[:, 0].reshape(BLOCK, HD),
        kv_last[:, 1].reshape(BLOCK, HD),
        same,
    )
    own_placing = placing(dests[local])
    staged_last[...] = (
        dot(own_placing.astype(BF), last).astype(BF).reshape(4, CAP, HD)
    )
    last_sems = [copies.new() for _ in range(3)]
    for k in range(1, 4):
        to = (section + k) % 4
        copies.start(
            last_sems[k - 1],
            staged_last.at[to],
            slots.at[to % 2, section, :, last_columns],
            in_section(to),
        )
    last_own = local_copy(
        staged_last.at[section], slots.at[core, section, :, last_columns]
    )

    def place_tile(tile, carry):
        placed = dot(placing(dests[tile]).astype(BF), mixed[tile]).astype(BF)
        staged[tile // 4, :, tile % 4] = placed.reshape(4, CAP, OWN)
        return carry

    lax.fori_loop(0, 8, place_tile, 0)
    slot_sems = [copies.new() for _ in range(7)]
    own_columns = pl.ds(pl.multiple_of(local * OWN, HD), OWN)
    for k in range(1, 8):
        to = (local + k) % 8
        copies.start(
            slot_sems[k - 1],
            staged.at[to // 4, to % 4],
            slots.at[to % 2, :, :, own_columns],
            in_block(to),
        )
    slot_own = local_copy(
        staged.at[local // 4, local % 4], slots.at[core, :, :, own_columns]
    )
    advance()

    relay_sems = [copies.new() for _ in range(9)]

    def relay(index, columns):
        copies.start(
            relay_sems[index],
            slots.at[core, :, :, columns],
            slots.at[core, :, :, columns],
            sibling,
        )

    last_own.wait()
    for k in range(1, 4):
        source = (section - k + 4) % 4
        copies.arrive(
            last_sems[k - 1],
            slots.at[core, source, :, last_columns],
            in_section(source),
        )
    relay(8, last_columns)
    slot_own.wait()
    relay(0, own_columns)
    for k in range(1, 8):
        source = (local - k + 8) % 8
        columns = pl.ds(pl.multiple_of(source * OWN, HD), OWN)
        copies.arrive(
            slot_sems[k - 1], slots.at[core, :, :, columns], in_block(source)
        )
        relay(k, columns)
    for gather in gathers:
        for _ in gather:
            pass
    other_local = local + 1 - 2 * core
    for k in range(8):
        source = (other_local - k + 8) % 8
        columns = pl.ds(pl.multiple_of(source * OWN, HD), OWN)
        copies.arrive(relay_sems[k], slots.at[1 - core, :, :, columns], sibling)
    copies.arrive(relay_sems[8], slots.at[1 - core, :, :, last_columns], sibling)

    window_row = lax.broadcasted_iota(jnp.int32, (512, OWN), 0)
    window_column = lax.broadcasted_iota(jnp.int32, (512, OWN), 1)

    def reorder(group, carry):
        window = slots[
            :, :, :, pl.ds(pl.multiple_of(group * OWN, HD), 512)
        ].reshape(512, 512)
        moved = dot(
            window, one_hot(window_row == window_column + 16 * group)
        ).astype(BF)
        for i in range(3):
            lhs[:, pl.ds(pl.multiple_of(i * 1024 + group * HD, HD), HD)] = moved[
                :, i * HD : (i + 1) * HD
            ]
        return carry

    lax.fori_loop(0, 8, reorder, 0)
    lane = lax.broadcasted_iota(jnp.int32, (512, HD), 1) // 16
    tail = jnp.zeros((512, HD), F32)
    for group in range(8):
        piece = slots[:, :, :, OWN * (group + 1) : OWN * (group + 1) + HD]
        tail = jnp.where(lane == group, piece.reshape(512, HD).astype(F32), tail)
    lhs[:, LAST:] = tail.astype(BF)

    for copy in grad_own:
        copy.wait()
    for half in range(2):
        copies.arrive(
            grad_sems[half],
            grads.at[1 - core, :, pl.ds(half * 2048, 2048)],
            sibling,
        )
    back[...] = jnp.zeros_like(back)

    def multiply(i, carry):
        low, x = i // 4, i % 4
        column = (low % 2) * 2048 + ((low // 2) * 4 + x) * COLS
        columns = pl.ds(pl.multiple_of(column, COLS), COLS)
        grad = grads[:, :, columns].reshape(512, COLS)
        total = jnp.zeros((512, COLS), F32)
        for first, rows, start in K_PARTS:
            rhs = weight[:, :, low, x, pl.ds(first, rows), :].reshape(8 * rows, COLS)
            depth = pl.ds(start, 8 * rows)
            total = total + dot(lhs[:, depth], rhs)
            back[:, depth] += dot_nt(grad, rhs)
        embeds[:, :, columns] = total.astype(BF).reshape(2, 256, COLS)
        return carry

    embed_sems = [copies.new() for _ in range(4)]
    embed_own = []
    for low in range(4):
        lax.fori_loop(4 * low, 4 * low + 4, multiply, 0)
        half, quarter = low % 2, low // 2
        here = pl.ds(half * 2048 + quarter * 1024, 1024)
        there = pl.ds(
            pl.multiple_of((2 * half + core) * 2048 + quarter * 1024, 1024), 1024
        )
        copies.start(
            embed_sems[low],
            embeds.at[1 - core, :, here],
            embeds_ref.at[0, :, there],
            sibling,
        )
        embed_own.append(
            local_copy(embeds.at[core, :, here], embeds_ref.at[0, :, there])
        )
    copies.drain()

    half_rows = pl.ds(pl.multiple_of((1 - core) * 256, 256), 256)
    slots[0] = back[half_rows, :].astype(BF).reshape(4, CAP, DV)
    back_sem = copies.new()
    copies.start(back_sem, slots.at[0], back_in, sibling)
    copies.arrive(back_sem, back_in, sibling)
    half_rows = pl.ds(pl.multiple_of(core * 256, 256), 256)
    summed = back[half_rows, :] + back_in[...].reshape(256, DV).astype(F32)
    slots[1] = summed.astype(BF).reshape(4, CAP, DV)
    return_sems = [copies.new() for _ in range(3)]
    for k in range(1, 4):
        to = (section + k) % 4
        copies.start(
            return_sems[k - 1], slots.at[1, to], returned.at[section], in_section(to)
        )
    local_copy(slots.at[1, section], returned.at[section]).wait()
    for k in range(1, 4):
        source = (section - k + 4) % 4
        copies.arrive(return_sems[k - 1], returned.at[source], in_section(source))
    chosen = dot(
        own_placing.T.astype(BF), returned[...].reshape(256, DV)
    ).astype(BF)
    rows = pl.ds(0, TILE)
    back[rows, :] = jnp.zeros((TILE, DV), F32)
    lane = lax.broadcasted_iota(jnp.int32, (TILE, HD), 1) // 16
    tail = chosen[:, LAST:].astype(F32)
    source_lane = lax.broadcasted_iota(jnp.int32, (OWN, 512), 0)
    target_lane = lax.broadcasted_iota(jnp.int32, (OWN, 512), 1)
    for group in range(8):
        piece = jnp.concatenate(
            [chosen[:, i * 1024 + group * HD : i * 1024 + (group + 1) * HD] for i in range(3)],
            axis=1,
        )
        moved = dot(piece, one_hot(target_lane == source_lane + 16 * group))
        back[rows, group * OWN : group * OWN + 512] += moved
        back[rows, (group + 1) * OWN : (group + 1) * OWN + HD] += jnp.where(
            lane == group, tail, 0.0
        )
    vgrad_ref[...] = back[rows, :].astype(BF)

    for copy in embed_own:
        copy.wait()
    for low in range(4):
        half, quarter = low % 2, low // 2
        there = pl.ds(
            pl.multiple_of((2 * half + 1 - core) * 2048 + quarter * 1024, 1024), 1024
        )
        copies.arrive(embed_sems[low], embeds_ref.at[0, :, there], sibling)
    copies.drain()


def on_device(query_rows, key_rows, value_rows, image_lengths, dest_group, proj_weight, llm_grad):
    dest = jnp.broadcast_to(dest_group.reshape(1, TILE), (8, TILE))
    shard = jnp.pad(proj_weight, ((0, 64 - proj_weight.shape[0]), (0, 0)))
    any_ = pl.BlockSpec(memory_space=pl.ANY)
    vmem = pltpu.VMEM
    return pl.pallas_call(
        kernel,
        out_shape=(
            jax.ShapeDtypeStruct(llm_grad.shape, BF),
            jax.ShapeDtypeStruct(query_rows.shape, BF),
        ),
        in_specs=[pl.BlockSpec(memory_space=pltpu.SMEM)] + [any_] * 6,
        out_specs=(any_, pl.BlockSpec(memory_space=pltpu.VMEM)),
        scratch_shapes=[
            vmem((4, 2, 4, 4, ROWS, COLS), BF),
            vmem((8, 64, COLS), BF),
            vmem((8, 3, TILE, OWN), BF),
            vmem((8, 2, TILE, HD), BF),
            vmem((TILE, HD), BF),
            vmem((8, 8, TILE), jnp.int32),
            vmem((8, TILE, OWN), BF),
            vmem((2, 4, 4, CAP, OWN), BF),
            vmem((4, CAP, HD), BF),
            vmem((2, 4, CAP, DV), BF),
            vmem((512, DV), BF),
            vmem((2, 256, 4096), BF),
            vmem((2, 256, 4096), BF),
            vmem((512, DV), F32),
            vmem((4, CAP, DV), BF),
            vmem((4, CAP, DV), BF),
            pltpu.SemaphoreType.DMA((192,)),
            pltpu.SemaphoreType.DMA((192,)),
            pltpu.SemaphoreType.DMA((32,)),
        ],
        compiler_params=pltpu.CompilerParams(
            collective_id=0, has_side_effects=True, vmem_limit_bytes=64 * 1024 * 1024
        ),
    )(image_lengths, dest, query_rows, key_rows, value_rows, shard, llm_grad)


def solution(mesh):
    placed = (
        P(("mp", "section"), None),
        P(("mp", "section"), None),
        P(("mp", "section"), None),
        P(),
        P(("mp", "section"), None),
        P("mp", "section"),
        P("section", "mp", None),
    )
    return jax.shard_map(
        on_device,
        mesh=mesh,
        in_specs=placed,
        out_specs=(P("section", "mp", None), P(("mp", "section"), None)),
        check_vma=False,
    )
```

time: 450 us -> 264 us (0.59)
  Pallas kernels: 0 us -> 253 us
  waiting for transfers between devices: 181 us -> 0 us
  blocking collectives: 118 us -> 0 us
  matrix products: 49.7 us -> 0 us
  local copies, waits for them, and re-layouts: 45.6 us -> 9.88 us
  starting transfers between devices: 24.6 us -> 0 us
  other arithmetic: 16.4 us -> 0 us
  between operations: 14 us -> 0.65 us
    pallas_call x0 -> x1, Pallas kernels: none -> 253 us  [on_device(): pl.pallas_call(kernel, out_shape=(jax.ShapeDtypeStruct(llm_grad.shape, BF...]
    ppermute x6 -> x0, waiting for transfers between devices: 156 us -> none  [swapped(): lax.ppermute(value, axis, [(i, i ^ 1 << stride) for i in range(lax.axis_s...]
    all_to_all x2 -> x0, blocking collectives: 118 us -> none  [the longest x1 66 us: on_device(): lax.all_to_all(outgoing.reshape(groups, capacity, full_cols), 'section',...]
    dot_general x12 -> x0, matrix products: 49.7 us -> none  [the longest x4 13 us: one_head(): jnp.dot(weights_bf, triple[2], preferred_element_type=jnp.float32)]
    all_to_all x2 -> x0, waiting for transfers between devices: 24.6 us -> none  [the longest x1 24.6 us: on_device(): lax.all_to_all(own_grad, 'section', split_axis=1, concat_axis=0, tiled=True)]
    unnamed x13 -> x5, local copies, waits for them, and re-layouts: 26 us -> 6.97 us
    ppermute x6 -> x0, starting transfers between devices: 14.9 us -> none  [swapped(): lax.ppermute(value, axis, [(i, i ^ 1 << stride) for i in range(lax.axis_s...]
    all_to_all x2 -> x0, starting transfers between devices: 9.59 us -> none  [the longest x1 5.64 us: on_device(): lax.all_to_all(llm_grad.reshape(groups, capacity, full_cols), 'section',...]
  transfers between devices with their start and end apart: 11 -> 0, of which waited for: 7 -> 0; matrix products, arithmetic and copies ran while one was open for 23% -> 0% of each run, Pallas kernels for 0% -> 0%
where the time goes in v1:
time: 264 us; the launch traced here: 263 us
  Pallas kernels  253 us (96%)
  local copies, waits for them, and re-layouts  9.88 us (4%)
    pallas_call x1, Pallas kernels, on_device(): pl.pallas_call(kernel, out_shape=(jax.ShapeDtypeStruct(llm_grad.shape, BF...  253 us
    unnamed x5, local copies, waits for them, and re-layouts  6.97 us

profile of v1, /device:TPU:1, one launch (start us, length us, event | category | flops | bytes accessed | tf_op | source)
XLA Modules:
  0.0 263.2 jit_solution(645683967641333203)
XLA Ops:
  0.6 1.2 broadcast_in_dim.8.dest_ref
  1.9 1.4 copy.9.lengths
  3.2 1.7 pad.4.w_ref
  4.9 252.6 %shard_map.86 = (bf16[1,256,8192]{2,1,0:T(8,128)(2,1)}, bf16[128,3200]{1,0:T(8,128)(2,1)}) custom-call(s32[32,3]{1,0:T(8,128)} %copy.9.lengths, s32[8,128]{1,0:T(8,128)} %broadcast_in_dim.8.dest_ref, bf16[128,3200]{1,0:T(8,128)(2,1)} %q_ref.1, bf16[128,3200]{1,0:T(8,128)(2,1)} %k_ref.1, bf16[128,3200]{1,0:T(8,128)(2,1)} %v_ref.1, ...), custom_call_target="tpu_custom_call" | custom-call | tf_op jit(solution)/shard_map/pallas_call | solution.py:551
  257.6 0.0 copy-start
  257.6 4.7 %copy.12 = bf16[1,256,8192]{2,1,0:T(8,128)(2,1)} copy(bf16[1,256,8192]{2,1,0:T(8,128)(2,1)} %get-tuple-element.4) | data formatting | bytes 8388608
  262.3 0.0 copy-done
  262.3 0.9 copy.13
Async XLA Ops:
  257.6 4.7 %copy-start = (bf16[128,3200]{1,0:T(8,128)(2,1)S(1)}, bf16[128,3200]{1,0:T(8,128)(2,1)}, u32[]{:S(2)}) copy-start(bf16[128,3200]{1,0:T(8,128)(2,1)} %get-tuple-element.5) | copy-start | bytes 2457604

commit v2 on v1

--- a/solution.py
+++ b/solution.py
@@ -130,6 +130,26 @@
     for axis in order:
         size = SIZES[axis]
         even = 1 - 2 * (me[axis] % 2)
+        if not done:
+            def tile_at(offset):
+                at = {a: me[a] for a in SIZES}
+                at[axis] = (me[axis] + offset * even + size) % size
+                spot = (at["y"], at["z"] // 4, at["z"] % 4, at["x"])
+                return buf.at[(*spot, pl.ds(first, rows), slice(None))], device(
+                    {**me, axis: at[axis]}
+                )
+
+            indices = [copies.new() for _ in range(size)]
+            for offset in range(1, size):
+                copies.start(
+                    indices[offset], tile_at(0)[0], tile_at(0)[0], tile_at(offset)[1]
+                )
+            yield
+            for offset in range(1, size):
+                index = indices[offset if offset % 2 else size - offset]
+                copies.arrive(index, *tile_at(offset))
+            done = [axis]
+            continue
         step = -even if flip else even
         near = {**me, axis: (me[axis] + step + size) % size}
         far = {**me, axis: (me[axis] - step + size) % size}
@@ -168,14 +188,16 @@
 
 def kernel(
     lengths,
-    dest_ref,
+    dest_col,
     q_ref,
     k_ref,
     v_ref,
-    w_ref,
+    w_rows,
     grad_ref,
     embeds_ref,
     vgrad_ref,
+    w_ref,
+    dest_ref,
     weight,
     w_pieces,
     qkv,
@@ -216,11 +238,21 @@
     greeted = [in_block((local + k) % 8) for k in range(1, 8)]
     greeted += [in_octet((member + k) % 8) for k in range(1, 8)]
     for axis, size in SIZES.items():
-        for step in (1, size - 1):
+        for step in range(1, size):
             greeted.append(device({**me, axis: (me[axis] + step) % size}))
     barrier = pltpu.get_barrier_semaphore()
     for other in greeted:
         pl.semaphore_signal(barrier, inc=1, device_id=other, device_id_type=MESH)
+    across = lax.broadcasted_iota(jnp.int32, (64, 50), 1)
+    down = lax.broadcasted_iota(jnp.int32, (64, 50), 0)
+    w_ref[...] = dot(one_hot(across == down), w_rows[...]).astype(BF)
+    diagonal = lax.broadcasted_iota(jnp.int32, (TILE, TILE), 0) == (
+        lax.broadcasted_iota(jnp.int32, (TILE, TILE), 1)
+    )
+    turned = jnp.sum(
+        jnp.where(diagonal, dest_col[...].astype(F32), 0.0), axis=0, keepdims=True
+    )
+    dest_ref[...] = jnp.broadcast_to(turned, (8, TILE)).astype(jnp.int32)
     pl.semaphore_wait(barrier, len(greeted))
 
     locals_ = []
@@ -308,7 +340,7 @@
         local_copy(grad_ref.at[0, :, here], grads.at[core, :, into])
     grad_own = locals_[-2:]
 
-    for _ in range(6):
+    for _ in range(3):
         advance()
 
     for copy in head_own:
@@ -326,7 +358,7 @@
     ends = []
     total = 0
     for i in range(3):
-        total = total + lengths[block, i]
+        total = total + lengths[i, block]
         ends.append(total)
     key_segments = segments((1, BLOCK), 1, 0, ends)
 
@@ -340,8 +372,14 @@
         mixed[tiles, :, columns] = attend(q, k, v, same).reshape(2, TILE, HD)
         return carry
 
+    def advance_z():
+        for gather in gathers[:2]:
+            next(gather, None)
+
+    advance_z()
     for head in range(3):
         lax.fori_loop(4 * head, 4 * head + 4, attend_chunk, 0)
+    advance_z()
     same = segments((TILE, 1), 0, local * TILE, ends) == key_segments
     last = attend(
         q_last[...],
@@ -459,24 +497,65 @@
         )
     back[...] = jnp.zeros_like(back)
 
-    def multiply(i, carry):
+    def chunk(i):
         low, x = i // 4, i % 4
         column = (low % 2) * 2048 + ((low // 2) * 4 + x) * COLS
         columns = pl.ds(pl.multiple_of(column, COLS), COLS)
+        return low, x, columns
+
+    def weight_rows(first, rows, low, x):
+        return weight[:, :, low, x, pl.ds(first, rows), :].reshape(8 * rows, COLS)
+
+    def multiply_back(i, carry):
+        low, x, columns = chunk(i)
         grad = grads[:, :, columns].reshape(512, COLS)
+        for first, rows, start in K_PARTS:
+            back[:, pl.ds(start, 8 * rows)] += dot_nt(
+                grad, weight_rows(first, rows, low, x)
+            )
+        return carry
+
+    def multiply(i, carry):
+        low, x, columns = chunk(i)
         total = jnp.zeros((512, COLS), F32)
         for first, rows, start in K_PARTS:
-            rhs = weight[:, :, low, x, pl.ds(first, rows), :].reshape(8 * rows, COLS)
-            depth = pl.ds(start, 8 * rows)
-            total = total + dot(lhs[:, depth], rhs)
-            back[:, depth] += dot_nt(grad, rhs)
+            total = total + dot(
+                lhs[:, pl.ds(start, 8 * rows)], weight_rows(first, rows, low, x)
+            )
         embeds[:, :, columns] = total.astype(BF).reshape(2, 256, COLS)
         return carry
+
+    copies.drain()
+    lax.fori_loop(0, 16, multiply_back, 0)
+
+    half_rows = pl.ds(pl.multiple_of((1 - core) * 256, 256), 256)
+    slots[0] = back[half_rows, :].astype(BF).reshape(4, CAP, DV)
+    back_sem = copies.new()
+    copies.start(back_sem, slots.at[0], back_in, sibling)
+    return_sems = [copies.new() for _ in range(3)]
+    returned_own = []
+
+    def add_back():
+        copies.arrive(back_sem, back_in, sibling)
+        half_rows = pl.ds(pl.multiple_of(core * 256, 256), 256)
+        summed = back[half_rows, :] + back_in[...].reshape(256, DV).astype(F32)
+        slots[1] = summed.astype(BF).reshape(4, CAP, DV)
+        for k in range(1, 4):
+            to = (section + k) % 4
+            copies.start(
+                return_sems[k - 1],
+                slots.at[1, to],
+                returned.at[section],
+                in_section(to),
+            )
+        returned_own.append(local_copy(slots.at[1, section], returned.at[section]))
 
     embed_sems = [copies.new() for _ in range(4)]
     embed_own = []
     for low in range(4):
         lax.fori_loop(4 * low, 4 * low + 4, multiply, 0)
+        if low == 1:
+            add_back()
         half, quarter = low % 2, low // 2
         here = pl.ds(half * 2048 + quarter * 1024, 1024)
         there = pl.ds(
@@ -491,23 +570,7 @@
         embed_own.append(
             local_copy(embeds.at[core, :, here], embeds_ref.at[0, :, there])
         )
-    copies.drain()
-
-    half_rows = pl.ds(pl.multiple_of((1 - core) * 256, 256), 256)
-    slots[0] = back[half_rows, :].astype(BF).reshape(4, CAP, DV)
-    back_sem = copies.new()
-    copies.start(back_sem, slots.at[0], back_in, sibling)
-    copies.arrive(back_sem, back_in, sibling)
-    half_rows = pl.ds(pl.multiple_of(core * 256, 256), 256)
-    summed = back[half_rows, :] + back_in[...].reshape(256, DV).astype(F32)
-    slots[1] = summed.astype(BF).reshape(4, CAP, DV)
-    return_sems = [copies.new() for _ in range(3)]
-    for k in range(1, 4):
-        to = (section + k) % 4
-        copies.start(
-            return_sems[k - 1], slots.at[1, to], returned.at[section], in_section(to)
-        )
-    local_copy(slots.at[1, section], returned.at[section]).wait()
+    returned_own[0].wait()
     for k in range(1, 4):
         source = (section - k + 4) % 4
         copies.arrive(return_sems[k - 1], returned.at[source], in_section(source))
@@ -544,9 +607,8 @@
 
 
 def on_device(query_rows, key_rows, value_rows, image_lengths, dest_group, proj_weight, llm_grad):
-    dest = jnp.broadcast_to(dest_group.reshape(1, TILE), (8, TILE))
-    shard = jnp.pad(proj_weight, ((0, 64 - proj_weight.shape[0]), (0, 0)))
     any_ = pl.BlockSpec(memory_space=pl.ANY)
+    in_vmem = pl.BlockSpec(memory_space=pltpu.VMEM)
     vmem = pltpu.VMEM
     return pl.pallas_call(
         kernel,
@@ -554,9 +616,11 @@
             jax.ShapeDtypeStruct(llm_grad.shape, BF),
             jax.ShapeDtypeStruct(query_rows.shape, BF),
         ),
-        in_specs=[pl.BlockSpec(memory_space=pltpu.SMEM)] + [any_] * 6,
+        in_specs=[pl.BlockSpec(memory_space=pltpu.SMEM), in_vmem, any_, any_, any_, in_vmem, any_],
         out_specs=(any_, pl.BlockSpec(memory_space=pltpu.VMEM)),
         scratch_shapes=[
+            vmem((64, 2048), BF),
+            vmem((8, TILE), jnp.int32),
             vmem((4, 2, 4, 4, ROWS, COLS), BF),
             vmem((8, 64, COLS), BF),
             vmem((8, 3, TILE, OWN), BF),
@@ -580,7 +644,7 @@
         compiler_params=pltpu.CompilerParams(
             collective_id=0, has_side_effects=True, vmem_limit_bytes=64 * 1024 * 1024
         ),
-    )(image_lengths, dest, query_rows, key_rows, value_rows, shard, llm_grad)
+    )(image_lengths.T, dest_group, query_rows, key_rows, value_rows, proj_weight, llm_grad)
 
 
 def solution(mesh):

time: 264 us -> 245 us (0.928)
  Pallas kernels: 253 us -> 237 us
  local copies, waits for them, and re-layouts: 9.88 us -> 7 us
    pallas_call x1, Pallas kernels: 253 us -> 237 us  [on_device(): pl.pallas_call(kernel, out_shape=(jax.ShapeDtypeStruct(llm_grad.shape, BF...]
where the time goes in v2:
time: 245 us
  Pallas kernels  237 us (97%)
  local copies, waits for them, and re-layouts  7 us (3%)
    pallas_call x1, Pallas kernels, on_device(): pl.pallas_call(kernel, out_shape=(jax.ShapeDtypeStruct(llm_grad.shape, BF...  237 us
    unnamed x5, local copies, waits for them, and re-layouts  7 us

profile of v2, /device:TPU:1, one launch (start us, length us, event | category | flops | bytes accessed | tf_op | source)
XLA Modules:
  0.0 245.0 jit_solution(10467502838731946063)
XLA Ops:
  0.6 1.4 copy.9.dest_col
  2.0 237.4 %shard_map.86 = (bf16[1,256,8192]{2,1,0:T(8,128)(2,1)}, bf16[128,3200]{1,0:T(8,128)(2,1)}) custom-call(s32[3,32]{1,0:T(4,128)} %bitcast.1, s32[128,1]{1,0:T(8,128)} %copy.9.dest_col, bf16[128,3200]{1,0:T(8,128)(2,1)} %q_ref.1, bf16[128,3200]{1,0:T(8,128)(2,1)} %k_ref.1, bf16[128,3200]{1,0:T(8,128)(2,1)} %v_ref.1, bf16[50,2048]{1,0:T(8,128)(2,1)} %w_rows.1, ...), custom_call_target="tpu_custom_call" | custom-call | tf_op jit(solution)/shard_map/pallas_call | solution.py:613
  239.4 0.0 copy-start
  239.4 4.7 %copy.12 = bf16[1,256,8192]{2,1,0:T(8,128)(2,1)} copy(bf16[1,256,8192]{2,1,0:T(8,128)(2,1)} %get-tuple-element.4) | data formatting | bytes 8388608
  244.1 0.0 copy-done
  244.1 0.9 copy.13
Async XLA Ops:
  239.4 4.7 %copy-start = (bf16[128,3200]{1,0:T(8,128)(2,1)S(1)}, bf16[128,3200]{1,0:T(8,128)(2,1)}, u32[]{:S(2)}) copy-start(bf16[128,3200]{1,0:T(8,128)(2,1)} %get-tuple-element.5) | copy-start | bytes 2457604

commit v3 on v2

--- a/solution.py
+++ b/solution.py
@@ -453,9 +453,7 @@
             slot_sems[k - 1], slots.at[core, :, :, columns], in_block(source)
         )
         relay(k, columns)
-    for gather in gathers:
-        for _ in gather:
-            pass
+    advance_z()
     other_local = local + 1 - 2 * core
     for k in range(8):
         source = (other_local - k + 8) % 8
@@ -525,6 +523,9 @@
         embeds[:, :, columns] = total.astype(BF).reshape(2, 256, COLS)
         return carry
 
+    for gather in gathers:
+        for _ in gather:
+            pass
     copies.drain()
     lax.fori_loop(0, 16, multiply_back, 0)
 

time: 245 us -> 241 us (0.984)
  Pallas kernels: 237 us -> 233 us
    pallas_call x1, Pallas kernels: 237 us -> 233 us  [on_device(): pl.pallas_call(kernel, out_shape=(jax.ShapeDtypeStruct(llm_grad.shape, BF...]
where the time goes in v3:
time: 241 us
  Pallas kernels  233 us (97%)
  local copies, waits for them, and re-layouts  7 us (3%)
    pallas_call x1, Pallas kernels, on_device(): pl.pallas_call(kernel, out_shape=(jax.ShapeDtypeStruct(llm_grad.shape, BF...  233 us
    unnamed x5, local copies, waits for them, and re-layouts  7 us

profile of v3, /device:TPU:1, one launch (start us, length us, event | category | flops | bytes accessed | tf_op | source)
XLA Modules:
  0.0 240.6 jit_solution(11847525902798682350)
XLA Ops:
  0.6 1.4 copy.9.dest_col
  2.0 233.0 %shard_map.86 = (bf16[1,256,8192]{2,1,0:T(8,128)(2,1)}, bf16[128,3200]{1,0:T(8,128)(2,1)}) custom-call(s32[3,32]{1,0:T(4,128)} %bitcast.1, s32[128,1]{1,0:T(8,128)} %copy.9.dest_col, bf16[128,3200]{1,0:T(8,128)(2,1)} %q_ref.1, bf16[128,3200]{1,0:T(8,128)(2,1)} %k_ref.1, bf16[128,3200]{1,0:T(8,128)(2,1)} %v_ref.1, bf16[50,2048]{1,0:T(8,128)(2,1)} %w_rows.1, ...), custom_call_target="tpu_custom_call" | custom-call | tf_op jit(solution)/shard_map/pallas_call | solution.py:614
  235.0 0.0 copy-start
  235.0 4.7 %copy.12 = bf16[1,256,8192]{2,1,0:T(8,128)(2,1)} copy(bf16[1,256,8192]{2,1,0:T(8,128)(2,1)} %get-tuple-element.4) | data formatting | bytes 8388608
  239.7 0.0 copy-done
  239.7 0.9 copy.13
Async XLA Ops:
  235.0 4.7 %copy-start = (bf16[128,3200]{1,0:T(8,128)(2,1)S(1)}, bf16[128,3200]{1,0:T(8,128)(2,1)}, u32[]{:S(2)}) copy-start(bf16[128,3200]{1,0:T(8,128)(2,1)} %get-tuple-element.5) | copy-start | bytes 2457604
